TPU v7x, 32 devices: a whole 2x2x4 slice. The times are simulated.
32 devices in a mesh: expert: 4 (over z), tensor: 8 (over y, x, core).
Axes of the slice: x: 2, y: 2, z: 4, core: 2. Of those that a mesh axis runs over, the one named last changes fastest.
Arguments:
- activations: bfloat16 [3072, 512], P('tensor', 'expert'), may hold values from -6 to 6
- cotangent: bfloat16 [3072, 512], P('tensor', 'expert'), may hold values from -4 to 4
- route_ids: int32 [512, 2], P('expert'), may hold values from 0 to 3, all different within a row; in each aligned block of 128 rows (0 to 127, 128 to 255, ...) at most 80 rows name the same one
- gate_probs: float32 [512, 2], P('expert'), may hold values from 0.2 to 0.8
- gate_weight: bfloat16 [4, 3072, 16384], P('expert', None, 'tensor'), may hold values from -0.15625 to 0.15625
- up_weight: bfloat16 [4, 3072, 16384], P('expert', None, 'tensor'), may hold values from -0.15625 to 0.15625
- down_weight: bfloat16 [4, 16384, 3072], P('expert', 'tensor'), may hold values from -0.046875 to 0.046875
Outputs:
- grad_input: bfloat16 [3072, 512], P('tensor', 'expert')
- score_grad: float32 [512, 2], P('expert')
Inputs may be any that keep to these rules, and one draw needn't show every extreme that they name: `route_ids`: each token names 2 different experts. Among the 128 tokens of one index of the expert axis no expert is named more than 80 times, and in every draw some such block names one expert exactly 80 times.
All inputs are finite; a program needn't handle non-finite values.
Results may differ from a plain program's by a relative error of at most 0.008.
Values may be sent and summed in bfloat16 or wider, within the bound.
A program may use at most 128 MiB of HBM per device.

v0:
```python
import jax
import jax.numpy as jnp
from jax import lax
from jax.sharding import PartitionSpec as P


def slot_numbers(route_ids, expert_count, capacity):
    token_count = route_ids.shape[0]
    onehot = (
        route_ids[:, :, None] == jnp.arange(expert_count, dtype=jnp.int32)[None, None, :]
    ).astype(jnp.int32)
    flattened = onehot.reshape(token_count * route_ids.shape[1], expert_count)
    earlier = jnp.cumsum(flattened, axis=0) - flattened
    position = jnp.sum(earlier * flattened, axis=1).reshape(route_ids.shape)
    return route_ids * capacity + position


def swiglu_backward(gate_sum, up_sum, hidden_grad):
    sigma = jax.nn.sigmoid(gate_sum)
    silu_value = gate_sum * sigma
    grad_up = (hidden_grad * silu_value).astype(jnp.bfloat16)
    grad_gate = (hidden_grad * up_sum * sigma * (1.0 + gate_sum * (1.0 - sigma))).astype(
        jnp.bfloat16
    )
    score_rows = jnp.sum(silu_value * up_sum * hidden_grad, axis=1)
    return (grad_gate, grad_up, score_rows)


def body(activations, cotangent, route_ids, gate_probs, gate_weight, up_weight, down_weight):
    expert_count = lax.axis_size("expert")
    tokens_here = route_ids.shape[0]
    capacity = min(tokens_here, 5 * tokens_here // (2 * expert_count))
    slot_total = expert_count * capacity
    destination = slot_numbers(route_ids, expert_count, capacity)
    slot_range = jnp.arange(slot_total, dtype=jnp.int32)
    matches = destination[:, :, None] == slot_range[None, None, :]
    placing = jnp.sum(matches.astype(jnp.float32), axis=1).astype(jnp.bfloat16)
    weighting = jnp.sum(jnp.where(matches, gate_probs[:, :, None], jnp.float32(0.0)), axis=1)
    gate_local = gate_weight[0]
    up_local = up_weight[0]
    down_local = down_weight[0]
    first_dims = (((0,), (0,)), ((), ()))
    down_dims = (((0,), (1,)), ((), ()))
    hidden_dims = (((1,), (1,)), ((), ()))
    send_in = jnp.dot(activations, placing, preferred_element_type=jnp.float32).astype(jnp.bfloat16)
    send_grad = jnp.dot(cotangent, placing, preferred_element_type=jnp.float32).astype(jnp.bfloat16)
    recv_in, recv_grad = (
        lax.all_to_all(send_in, "expert", split_axis=1, concat_axis=1, tiled=True),
        lax.all_to_all(send_grad, "expert", split_axis=1, concat_axis=1, tiled=True),
    )
    feature_piece = lax.all_gather(recv_in, "tensor", axis=0, tiled=True)
    grad_piece = lax.all_gather(recv_grad, "tensor", axis=0, tiled=True)
    gate_rows = gate_local
    up_rows = up_local
    gate_sum = lax.dot_general(
        feature_piece, gate_rows, first_dims, preferred_element_type=jnp.float32
    )
    up_sum = lax.dot_general(feature_piece, up_rows, first_dims, preferred_element_type=jnp.float32)
    hidden_grad = lax.dot_general(
        grad_piece, down_local, down_dims, preferred_element_type=jnp.float32
    )
    gate_sum, up_sum, hidden_grad = (gate_sum, up_sum, hidden_grad)
    grad_gate, grad_up, score_rows = swiglu_backward(gate_sum, up_sum, hidden_grad)
    gate_rows = gate_local
    up_rows = up_local
    term = lax.dot_general(gate_rows, grad_gate, hidden_dims, preferred_element_type=jnp.float32)
    term_slice = lax.psum_scatter(
        term + lax.dot_general(up_rows, grad_up, hidden_dims, preferred_element_type=jnp.float32),
        "tensor",
        scatter_dimension=0,
        tiled=True,
    )
    score_whole = lax.psum(score_rows[None, :], "tensor")
    back_terms, back_scores = (
        lax.all_to_all(term_slice, "expert", split_axis=1, concat_axis=1, tiled=True),
        lax.all_to_all(score_whole, "expert", split_axis=1, concat_axis=1, tiled=True),
    )
    grad_local = jnp.dot(
        back_terms, weighting.T, precision=lax.Precision.HIGHEST, preferred_element_type=jnp.float32
    )
    score_grad = jnp.sum(
        jnp.where(matches, back_scores[0][None, None, :], jnp.float32(0.0)), axis=2
    )
    grad_input = grad_local.astype(jnp.bfloat16)
    return (grad_input, score_grad)


def solution(mesh):
    in_specs = (
        P("tensor", "expert"),
        P("tensor", "expert"),
        P("expert", None),
        P("expert", None),
        P("expert", None, "tensor"),
        P("expert", None, "tensor"),
        P("expert", "tensor", None),
    )
    out_specs = (P("tensor", "expert"), P("expert", None))
    return jax.shard_map(body, mesh=mesh, in_specs=in_specs, out_specs=out_specs, check_vma=False)
```

profile of v0, /device:TPU:0, one launch (start us, length us, event | category | flops | bytes accessed | tf_op | source)
XLA Modules:
  0.0 196.6 jit_solution(7159178132124961180)
XLA Ops:
  7.2 0.0 copy-start
  7.2 0.0 all-gather.5.cloned.1.call-start
  7.2 0.8 copy.34
  8.0 0.1 eq.43
  8.2 0.1 eq.39
  8.3 1.2 reduce-window.6
  9.5 0.1 slice.8
  9.6 0.1 copy.36
  9.8 0.1 copy.37
  9.9 0.1 add_bitcast_fusion
  9.9 0.1 reshape.38
  10.1 0.1 copy.38
  10.2 0.7 multiply_add_fusion
  10.9 0.0 copy-done
  10.9 0.2 convolution_convert_fusion
  11.2 14.7 %all_to_all.45 = bf16[384,4,80]{0,2,1:T(8,128)(2,1)} all-to-all(bf16[384,4,80]{0,2,1:T(8,128)(2,1)S(1)} %bitcast.64), channel_id=1, replica_groups=mesh['expert'=4,'tensor'=8] {'expert'}, dimensions={1} | all-to-all | bytes 491520 | tf_op jit(solution)/shard_map/all_to_all | solution.py:48
  25.9 0.0 all-gather.5.cloned.1.call-update
  25.9 0.0 all-gather.3.cloned.1.call-start
  26.0 1.1 convolution_convert_fusion.1
  27.1 10.7 %all_to_all.46 = bf16[384,4,80]{0,2,1:T(8,128)(2,1)} all-to-all(bf16[384,4,80]{0,2,1:T(8,128)(2,1)S(1)} %bitcast.63), channel_id=1, replica_groups=mesh['expert'=4,'tensor'=8] {'expert'}, dimensions={1} | all-to-all | bytes 491520 | tf_op jit(solution)/shard_map/all_to_all | solution.py:49
  37.9 0.0 all-gather.3.cloned.1.call-update
  37.9 0.0 reduce-scatter.2.cloned.1.call-start
  37.9 14.9 %all-gather.5.cloned.1.call-done = bf16[3072,320]{0,1:T(8,128)(2,1)} async-done(((bf16[384,320]{0,1:T(8,128)(2,1)}), bf16[3072,320]{0,1:T(8,128)(2,1)}) %all-gather.5.cloned.1.call-update) | async-done | bytes 1966096 | tf_op jit(solution)/shard_map/all_gather | solution.py:51
  52.8 0.0 copy-start.2
  52.8 9.4 %fusion.2 = f32[320,2048]{1,0:T(8,128)S(1)} fusion(bf16[3072,320]{0,1:T(8,128)(2,1)} %all-gather.5.cloned.1.call-done, bf16[1,3072,2048]{2,1,0:T(8,128)(2,1)} %param.11), kind=kOutput, calls=%fused_computation.2 | convolution fusion | flops 4026531840 | bytes 17170432 | tf_op jit(solution)/shard_map/dot_general | solution.py:55
  62.2 0.0 copy-done.2
  62.2 8.9 %fusion.6 = f32[320,2048]{1,0:T(8,128)} fusion(bf16[3072,320]{0,1:T(8,128)(2,1)S(1)} %copy-done.2, bf16[1,3072,2048]{2,1,0:T(8,128)(2,1)} %param.12), kind=kOutput, calls=%fused_computation.6 | convolution fusion | flops 4026531840 | bytes 17170432 | tf_op jit(solution)/shard_map/dot_general | solution.py:58
  71.1 11.3 %all-gather.3.cloned.1.call-done = bf16[3072,320]{0,1:T(8,128)(2,1)} async-done(((bf16[384,320]{0,1:T(8,128)(2,1)}), bf16[3072,320]{0,1:T(8,128)(2,1)}) %all-gather.3.cloned.1.call-update) | async-done | bytes 1966096 | tf_op jit(solution)/shard_map/all_gather | solution.py:52
  82.3 12.0 %multiply_reduce_fusion = (f32[320]{0:T(512)S(1)}, f32[320,2048]{1,0:T(8,128)}) fusion(f32[320,2048]{1,0:T(8,128)} %fusion.6, f32[320,2048]{1,0:T(8,128)S(1)} %fusion.2, bf16[3072,320]{0,1:T(8,128)(2,1)} %all-gather.3.cloned.1.call-done, bf16[1,2048,3072]{2,1,0:T(8,128)(2,1)} %param.13), kind=kOutput, calls=%fused_computation.12 | convolution fusion | flops 4031119104 | bytes 22414592 | tf_op jit(solution)/shard_map/dot_general | solution.py:59
  94.3 12.7 %fusion = f32[320,3072]{1,0:T(8,128)} fusion(bf16[1,3072,2048]{2,1,0:T(8,128)(2,1)} %param.11, f32[320,2048]{1,0:T(8,128)S(1)} %fusion.2, f32[320,2048]{1,0:T(8,128)} %get-tuple-element.5, f32[320,2048]{1,0:T(8,128)} %fusion.6), kind=kOutput, calls=%fused_computation | convolution fusion | flops 4033085440 | bytes 24379392 | tf_op jit(solution)/shard_map/dot_general | solution.py:66
  107.0 12.6 %fusion.13 = f32[3072,320]{0,1:T(8,128)} fusion(f32[320,3072]{1,0:T(8,128)} %fusion, bf16[1,3072,2048]{2,1,0:T(8,128)(2,1)} %param.12, f32[320,2048]{1,0:T(8,128)} %get-tuple-element.5, f32[320,2048]{1,0:T(8,128)S(1)} %fusion.2), kind=kOutput, calls=%fused_computation.11 | convolution fusion | flops 4031447040 | bytes 25690112 | tf_op jit(solution)/shard_map/dot_general | solution.py:68
  119.7 0.0 copy-start.1
  119.7 0.0 reduce-scatter.2.cloned.1.call-update
  119.7 0.1 all_to_all.39
  119.8 13.1 %psum.7 = f32[1,4,80]{2,0,1:T(1,128)S(1)} all-reduce(f32[1,4,80]{2,0,1:T(1,128)S(1)} %all_to_all.39), channel_id=1, replica_groups=mesh['expert'=4,'tensor'=8] {'tensor'}, use_global_device_ids=true, to_apply=%region_7.8 | all-reduce | flops 320 | bytes 2560 | tf_op jit(solution)/shard_map/psum | solution.py:73
  132.9 9.9 %all_to_all.47 = f32[1,4,80]{2,0,1:T(1,128)S(1)} all-to-all(f32[1,4,80]{2,0,1:T(1,128)S(1)} %psum.7), channel_id=1, replica_groups=mesh['expert'=4,'tensor'=8] {'expert'}, dimensions={1} | all-to-all | bytes 2560 | tf_op jit(solution)/shard_map/all_to_all | solution.py:76
  142.8 27.1 %reduce-scatter.2.cloned.1.call-done = f32[384,320]{0,1:T(8,128)} async-done(((f32[3072,320]{0,1:T(8,128)}), f32[384,320]{0,1:T(8,128)}) %reduce-scatter.2.cloned.1.call-update) | async-done | bytes 491536 | tf_op jit(solution)/shard_map/reduce_scatter | solution.py:67
  169.9 4.6 %all-to-all-start.2 = ((f32[384,4,80]{0,2,1:T(8,128)}), f32[384,4,80]{0,2,1:T(8,128)S(1)}, u32[]{:S(2)}, u32[]{:S(2)}) async-start(f32[384,4,80]{0,2,1:T(8,128)} %bitcast.65), calls=%async_computation.3 | async-start | bytes 983040 | tf_op jit(solution)/shard_map/all_to_all | solution.py:75
  174.5 0.5 broadcast.35
  175.0 0.7 reduce.3
  175.7 0.1 broadcast_in_dim.35
  175.7 0.0 copy-done.1
  175.7 0.7 select_reduce_fusion
  176.4 11.8 %all-to-all-done.2 = f32[384,4,80]{0,2,1:T(8,128)S(1)} async-done(((f32[384,4,80]{0,2,1:T(8,128)}), f32[384,4,80]{0,2,1:T(8,128)S(1)}, u32[]{:S(2)}, u32[]{:S(2)}) %all-to-all-start.2) | async-done | bytes 491552 | tf_op jit(solution)/shard_map/all_to_all | solution.py:75
  188.3 1.8 convolution_convert_fusion.2
  (5 shorter events, 0.1 us)
Async XLA Ops:
  7.2 3.7 %copy-start = (bf16[384,128]{1,0:T(8,128)(2,1)S(1)}, bf16[384,128]{1,0:T(8,128)(2,1)}, u32[]{:S(2)}) copy-start(bf16[384,128]{1,0:T(8,128)(2,1)} %param.7) | copy-start | bytes 294916
  7.2 45.6 %all-gather.5.cloned.1.call-start = ((), (), s32[]{:S(2)}) async-start(), calls=%async_computation.6 | async-start | bytes 2211840 | tf_op jit(solution)/shard_map/all_gather | solution.py:51
  25.9 56.4 %all-gather.3.cloned.1.call-start = ((), (), s32[]{:S(2)}) async-start(), calls=%async_computation.5 | async-start | bytes 2211840 | tf_op jit(solution)/shard_map/all_gather | solution.py:52
  37.9 132.0 %reduce-scatter.2.cloned.1.call-start = ((), (), s32[]{:S(2)}) async-start(), calls=%async_computation.7 | async-start | bytes 4423680 | tf_op jit(solution)/shard_map/reduce_scatter | solution.py:67
  52.8 9.4 %copy-start.2 = (bf16[3072,320]{0,1:T(8,128)(2,1)S(1)}, bf16[3072,320]{0,1:T(8,128)(2,1)}, u32[]{:S(2)}) copy-start(bf16[3072,320]{0,1:T(8,128)(2,1)} %all-gather.5.cloned.1.call-done) | copy-start | bytes 5898244
  119.7 56.1 %copy-start.1 = (f32[128,2]{0,1:T(2,128)S(1)}, f32[128,2]{0,1:T(2,128)}, u32[]{:S(2)}) copy-start(f32[128,2]{0,1:T(2,128)} %param.10) | copy-start | bytes 3076
  169.9 18.4 %all-to-all-start.2 = ((f32[384,4,80]{0,2,1:T(8,128)}), f32[384,4,80]{0,2,1:T(8,128)S(1)}, u32[]{:S(2)}, u32[]{:S(2)}) async-start(f32[384,4,80]{0,2,1:T(8,128)} %bitcast.65), calls=%async_computation.3 | async-start | bytes 983040 | tf_op jit(solution)/shard_map/all_to_all | solution.py:75
Sparse Core Ops, SparseCore 0:
  26.1 26.7 all-gather.4
  54.7 27.6 all-gather.2
  119.8 50.0 reduce-scatter.1
where the time goes:
time: 197 us
  waiting for transfers between devices  65.1 us (33%)
  matrix products  58.7 us (30%)
  blocking collectives  48.5 us (25%)
  between operations  13.8 us (7%)
  starting transfers between devices  4.72 us (2%)
  other arithmetic  3.47 us (2%)
  local copies, waits for them, and re-layouts  2.24 us (1%)
    reduce_scatter x1, waiting for transfers between devices, body(): lax.psum_scatter(term + lax.dot_general(up_rows, grad_up, hidden_dims, pr...  27.1 us
    all_gather x1, waiting for transfers between devices, body(): feature_piece = lax.all_gather(recv_in, 'tensor', axis=0, tiled=True)  14.9 us
    all_to_all x1, blocking collectives, body(): lax.all_to_all(send_in, 'expert', split_axis=1, concat_axis=1, tiled=True)  14.7 us
    psum x1, blocking collectives, body(): score_whole = lax.psum(score_rows[None, :], 'tensor')  13.1 us
    dot_general x1, matrix products, body(): lax.dot_general(gate_rows, grad_gate, hidden_dims, preferred_element_type...  12.7 us
    dot_general x1, matrix products, body(): lax.dot_general(up_rows, grad_up, hidden_dims, preferred_element_type=jnp...  12.6 us
    dot_general x1, matrix products, body(): lax.dot_general(grad_piece, down_local, down_dims, preferred_element_type...  12 us
    all_to_all x1, waiting for transfers between devices, body(): lax.all_to_all(term_slice, 'expert', split_axis=1, concat_axis=1, tiled=T...  11.8 us
  transfers between devices with their start and end apart: 4, of which 4 were waited for; matrix products, arithmetic and copies ran while one was open for 11% of the time, Pallas kernels for 0%

commit v1 on v0

--- a/solution.py
+++ b/solution.py
@@ -4,14 +4,17 @@
 from jax.sharding import PartitionSpec as P
 
 
+EXTRA_ROWS = 16
+
+
 def slot_numbers(route_ids, expert_count, capacity):
     token_count = route_ids.shape[0]
-    onehot = (
-        route_ids[:, :, None] == jnp.arange(expert_count, dtype=jnp.int32)[None, None, :]
-    ).astype(jnp.int32)
-    flattened = onehot.reshape(token_count * route_ids.shape[1], expert_count)
-    earlier = jnp.cumsum(flattened, axis=0) - flattened
-    position = jnp.sum(earlier * flattened, axis=1).reshape(route_ids.shape)
+    onehot = route_ids[:, :, None] == jnp.arange(expert_count, dtype=jnp.int32)[None, None, :]
+    named = jnp.sum(onehot.astype(jnp.float32), axis=1).astype(jnp.bfloat16)
+    order = jnp.arange(token_count, dtype=jnp.int32)
+    before = (order[None, :] < order[:, None]).astype(jnp.bfloat16)
+    earlier = jnp.dot(before, named, preferred_element_type=jnp.float32)
+    position = jnp.sum(jnp.where(onehot, earlier[:, None, :], 0.0), axis=2).astype(jnp.int32)
     return route_ids * capacity + position
 
 
@@ -42,12 +45,11 @@
     first_dims = (((0,), (0,)), ((), ()))
     down_dims = (((0,), (1,)), ((), ()))
     hidden_dims = (((1,), (1,)), ((), ()))
-    send_in = jnp.dot(activations, placing, preferred_element_type=jnp.float32).astype(jnp.bfloat16)
-    send_grad = jnp.dot(cotangent, placing, preferred_element_type=jnp.float32).astype(jnp.bfloat16)
-    recv_in, recv_grad = (
-        lax.all_to_all(send_in, "expert", split_axis=1, concat_axis=1, tiled=True),
-        lax.all_to_all(send_grad, "expert", split_axis=1, concat_axis=1, tiled=True),
-    )
+    features_here = activations.shape[0]
+    both = jnp.concatenate([activations, cotangent], axis=0)
+    send = jnp.dot(both, placing, preferred_element_type=jnp.float32).astype(jnp.bfloat16)
+    recv = lax.all_to_all(send, "expert", split_axis=1, concat_axis=1, tiled=True)
+    recv_in, recv_grad = recv[:features_here], recv[features_here:]
     feature_piece = lax.all_gather(recv_in, "tensor", axis=0, tiled=True)
     grad_piece = lax.all_gather(recv_grad, "tensor", axis=0, tiled=True)
     gate_rows = gate_local
@@ -64,17 +66,29 @@
     gate_rows = gate_local
     up_rows = up_local
     term = lax.dot_general(gate_rows, grad_gate, hidden_dims, preferred_element_type=jnp.float32)
-    term_slice = lax.psum_scatter(
-        term + lax.dot_general(up_rows, grad_up, hidden_dims, preferred_element_type=jnp.float32),
-        "tensor",
-        scatter_dimension=0,
-        tiled=True,
+    term = term + lax.dot_general(
+        up_rows, grad_up, hidden_dims, preferred_element_type=jnp.float32
     )
-    score_whole = lax.psum(score_rows[None, :], "tensor")
-    back_terms, back_scores = (
-        lax.all_to_all(term_slice, "expert", split_axis=1, concat_axis=1, tiled=True),
-        lax.all_to_all(score_whole, "expert", split_axis=1, concat_axis=1, tiled=True),
+    tensor_count = lax.axis_size("tensor")
+    score_high = score_rows.astype(jnp.bfloat16)
+    score_low = (score_rows - score_high.astype(jnp.float32)).astype(jnp.bfloat16)
+    extra = jnp.concatenate(
+        [
+            score_high[None, :],
+            score_low[None, :],
+            jnp.zeros((EXTRA_ROWS - 2, slot_total), jnp.bfloat16),
+        ],
+        axis=0,
     )
+    blocks = term.astype(jnp.bfloat16).reshape(tensor_count, features_here, slot_total)
+    extra = jnp.broadcast_to(extra[None], (tensor_count, EXTRA_ROWS, slot_total))
+    summed = lax.psum_scatter(
+        jnp.concatenate([blocks, extra], axis=1), "tensor", scatter_dimension=0, tiled=False
+    )
+    back = lax.all_to_all(summed, "expert", split_axis=1, concat_axis=1, tiled=True)
+    back = back.astype(jnp.float32)
+    back_terms = back[:features_here]
+    back_scores = back[features_here : features_here + 1] + back[features_here + 1 : features_here + 2]
     grad_local = jnp.dot(
         back_terms, weighting.T, precision=lax.Precision.HIGHEST, preferred_element_type=jnp.float32
     )

time: 197 us -> 196 us (level)
  waiting for transfers between devices: 65.1 us -> 81.9 us
  blocking collectives: 48.5 us -> 34.8 us
  starting transfers between devices: 4.72 us -> 0.12 us
    reduce_scatter x1, waiting for transfers between devices: 27.1 us -> 43.8 us  [body(): lax.psum_scatter(jnp.concatenate([blocks, extra], axis=1), 'tensor', scat...]
    psum x1 -> x0, blocking collectives: 13.1 us -> none  [body(): score_whole = lax.psum(score_rows[None, :], 'tensor')]
    all_to_all x1 -> x0, waiting for transfers between devices: 11.8 us -> none  [body(): lax.all_to_all(term_slice, 'expert', split_axis=1, concat_axis=1, tiled=T...]
    all_gather x1, waiting for transfers between devices: 14.9 us -> 26 us  [body(): feature_piece = lax.all_gather(recv_in, 'tensor', axis=0, tiled=True)]
    all_to_all x1 -> x0, starting transfers between devices: 4.6 us -> none  [body(): lax.all_to_all(term_slice, 'expert', split_axis=1, concat_axis=1, tiled=T...]
    all_to_all x3 -> x2, blocking collectives: 35.4 us -> 34.8 us  [the longest x1 19.9 us: body(): lax.all_to_all(send, 'expert', split_axis=1, concat_axis=1, tiled=True)]
  transfers between devices with their start and end apart: 4 -> 3, of which waited for: 4 -> 3; matrix products, arithmetic and copies ran while one was open for 11% -> 9% of each run, Pallas kernels for 0% -> 0%
where the time goes in v1:
time: 196 us
  waiting for transfers between devices  81.9 us (42%)
  matrix products  57.2 us (29%)
  blocking collectives  34.8 us (18%)
  between operations  13.8 us (7%)
  other arithmetic  5.1 us (3%)
  local copies, waits for them, and re-layouts  3.01 us (2%)
    reduce_scatter x1, waiting for transfers between devices, body(): lax.psum_scatter(jnp.concatenate([blocks, extra], axis=1), 'tensor', scat...  43.8 us
    all_gather x1, waiting for transfers between devices, body(): feature_piece = lax.all_gather(recv_in, 'tensor', axis=0, tiled=True)  26 us
    all_to_all x1, blocking collectives, body(): lax.all_to_all(send, 'expert', split_axis=1, concat_axis=1, tiled=True)  19.9 us
    all_to_all x1, blocking collectives, body(): lax.all_to_all(summed, 'expert', split_axis=1, concat_axis=1, tiled=True)  14.9 us
    dot_general x1, matrix products, body(): lax.dot_general(gate_rows, grad_gate, hidden_dims, preferred_element_type...  12.7 us
    dot_general x1, matrix products, body(): lax.dot_general(up_rows, grad_up, hidden_dims, preferred_element_type=jnp...  12 us
    dot_general x1, matrix products, body(): lax.dot_general(grad_piece, down_local, down_dims, preferred_element_type...  11.9 us
    all_gather x1, waiting for transfers between devices, body(): grad_piece = lax.all_gather(recv_grad, 'tensor', axis=0, tiled=True)  11.3 us
  transfers between devices with their start and end apart: 3, of which 3 were waited for; matrix products, arithmetic and copies ran while one was open for 9% of the time, Pallas kernels for 0%

profile of v1, /device:TPU:0, one launch (start us, length us, event | category | flops | bytes accessed | tf_op | source)
XLA Modules:
  0.0 195.9 jit_solution(15197801088992808342)
XLA Ops:
  7.2 0.0 all-gather.5.cloned.1.call-start
  7.2 0.7 convert_reduce_fusion.1
  7.9 0.1 fusion.24
  8.0 0.7 select_reduce_fusion.2
  8.8 0.7 convert_add_fusion
  9.5 1.2 convolution_convert_fusion
  10.7 19.9 %all_to_all.18 = bf16[768,4,80]{0,2,1:T(8,128)(2,1)S(1)} all-to-all(bf16[768,4,80]{0,2,1:T(8,128)(2,1)S(1)} %bitcast.38), channel_id=1, replica_groups=mesh['expert'=4,'tensor'=8] {'expert'}, dimensions={1} | all-to-all | bytes 983040 | tf_op jit(solution)/shard_map/all_to_all | solution.py:51
  30.6 0.8 fusion.29
  31.5 0.0 all-gather.5.cloned.1.call-update
  31.5 0.0 all-gather.3.cloned.1.call-start
  31.5 0.7 all-gather.3.cloned.1.call-update
  32.2 0.0 reduce-scatter.2.cloned.1.call-start
  32.3 0.1 pad.4.clone
  32.4 26.0 %all-gather.5.cloned.1.call-done = bf16[3072,320]{0,1:T(8,128)(2,1)} async-done(((bf16[384,320]{0,1:T(8,128)(2,1)}), bf16[3072,320]{0,1:T(8,128)(2,1)}) %all-gather.5.cloned.1.call-update) | async-done | bytes 1966096 | tf_op jit(solution)/shard_map/all_gather | solution.py:53
  58.4 0.0 copy-start.1
  58.4 9.4 %fusion.2 = f32[320,2048]{1,0:T(8,128)S(1)} fusion(bf16[3072,320]{0,1:T(8,128)(2,1)} %all-gather.5.cloned.1.call-done, bf16[1,3072,2048]{2,1,0:T(8,128)(2,1)} %param.11), kind=kOutput, calls=%fused_computation.2 | convolution fusion | flops 4026531840 | bytes 17170432 | tf_op jit(solution)/shard_map/dot_general | solution.py:57
  67.7 0.0 copy-done.1
  67.7 8.8 %fusion.6 = f32[320,2048]{1,0:T(8,128)} fusion(bf16[3072,320]{0,1:T(8,128)(2,1)S(1)} %copy-done.1, bf16[1,3072,2048]{2,1,0:T(8,128)(2,1)} %param.12), kind=kOutput, calls=%fused_computation.6 | convolution fusion | flops 4026531840 | bytes 17170432 | tf_op jit(solution)/shard_map/dot_general | solution.py:60
  76.5 11.3 %all-gather.3.cloned.1.call-done = bf16[3072,320]{0,1:T(8,128)(2,1)} async-done(((bf16[384,320]{0,1:T(8,128)(2,1)}), bf16[3072,320]{0,1:T(8,128)(2,1)}) %all-gather.3.cloned.1.call-update) | async-done | bytes 1966096 | tf_op jit(solution)/shard_map/all_gather | solution.py:54
  87.9 11.9 %multiply_reduce_fusion = (f32[320]{0:T(512)S(1)}, f32[320,2048]{1,0:T(8,128)}) fusion(f32[320,2048]{1,0:T(8,128)} %fusion.6, f32[320,2048]{1,0:T(8,128)S(1)} %fusion.2, bf16[3072,320]{0,1:T(8,128)(2,1)} %all-gather.3.cloned.1.call-done, bf16[1,2048,3072]{2,1,0:T(8,128)(2,1)} %param.13), kind=kOutput, calls=%fused_computation.13 | convolution fusion | flops 4031119104 | bytes 22414592 | tf_op jit(solution)/shard_map/dot_general | solution.py:61
  99.8 12.7 %fusion = f32[320,3072]{1,0:T(8,128)} fusion(bf16[1,3072,2048]{2,1,0:T(8,128)(2,1)} %param.11, f32[320,2048]{1,0:T(8,128)S(1)} %fusion.2, f32[320,2048]{1,0:T(8,128)} %get-tuple-element.7, f32[320,2048]{1,0:T(8,128)} %fusion.6), kind=kOutput, calls=%fused_computation | convolution fusion | flops 4033085440 | bytes 24379392 | tf_op jit(solution)/shard_map/dot_general | solution.py:68
  112.5 12.0 %fusion.13 = bf16[320,3072]{1,0:T(8,128)(2,1)} fusion(f32[320,3072]{1,0:T(8,128)} %fusion, bf16[1,3072,2048]{2,1,0:T(8,128)(2,1)} %param.12, f32[320,2048]{1,0:T(8,128)} %get-tuple-element.7, f32[320,2048]{1,0:T(8,128)S(1)} %fusion.2), kind=kOutput, calls=%fused_computation.11 | convolution fusion | flops 4032430080 | bytes 23724032 | tf_op jit(solution)/shard_map/dot_general | solution.py:69
  124.5 1.8 copy.30
  126.2 0.1 maximum_maximum_fusion
  126.3 0.1 copy.26
  126.4 0.1 broadcast_in_dim.58
  126.5 1.9 pad_maximum_fusion
  128.4 0.0 copy-start
  128.4 0.0 reduce-scatter.2.cloned.1.call-update
  128.4 43.8 %reduce-scatter.2.cloned.1.call-done = bf16[1,400,320]{1,2,0:T(8,128)(2,1)} async-done(((bf16[8,400,320]{1,2,0:T(8,128)(2,1)}), bf16[1,400,320]{1,2,0:T(8,128)(2,1)}) %reduce-scatter.2.cloned.1.call-update) | async-done | bytes 256016 | tf_op jit(solution)/shard_map/reduce_scatter | solution.py:85
  172.2 14.9 %all_to_all.19 = bf16[400,4,80]{0,2,1:T(8,128)(2,1)S(1)} all-to-all(bf16[400,4,80]{0,2,1:T(8,128)(2,1)} %bitcast.42), channel_id=1, replica_groups=mesh['expert'=4,'tensor'=8] {'expert'}, dimensions={1} | all-to-all | bytes 512000 | tf_op jit(solution)/shard_map/all_to_all | solution.py:88
  187.1 0.1 convert_element_type.86
  187.2 0.2 fusion.22
  187.4 0.1 broadcast_in_dim.61
  187.5 0.0 copy-done
  187.5 0.7 select_reduce_fusion
  188.2 1.2 convolution_convert_fusion.1
  (5 shorter events, 0.1 us)
Async XLA Ops:
  7.2 51.2 %all-gather.5.cloned.1.call-start = ((), (), s32[]{:S(2)}) async-start(), calls=%async_computation.4 | async-start | bytes 2211840 | tf_op jit(solution)/shard_map/all_gather | solution.py:53
  31.5 56.4 %all-gather.3.cloned.1.call-start = ((), (), s32[]{:S(2)}) async-start(), calls=%async_computation.3 | async-start | bytes 2211840 | tf_op jit(solution)/shard_map/all_gather | solution.py:54
  32.2 140.0 %reduce-scatter.2.cloned.1.call-start = ((), (), s32[]{:S(2)}) async-start(), calls=%async_computation.5 | async-start | bytes 2949120 | tf_op jit(solution)/shard_map/reduce_scatter | solution.py:85
  58.4 9.4 %copy-start.1 = (bf16[3072,320]{0,1:T(8,128)(2,1)S(1)}, bf16[3072,320]{0,1:T(8,128)(2,1)}, u32[]{:S(2)}) copy-start(bf16[3072,320]{0,1:T(8,128)(2,1)} %all-gather.5.cloned.1.call-done) | copy-start | bytes 5898244
  128.4 59.1 %copy-start = (f32[128,2]{0,1:T(2,128)S(1)}, f32[128,2]{0,1:T(2,128)}, u32[]{:S(2)}) copy-start(f32[128,2]{0,1:T(2,128)} %param.10) | copy-start | bytes 3076
Sparse Core Ops, SparseCore 0:
  31.6 26.7 all-gather.4
  60.2 27.6 all-gather.2
  128.5 43.6 reduce-scatter.1

commit v2 on v1

--- a/solution.py
+++ b/solution.py
@@ -4,7 +4,7 @@
 from jax.sharding import PartitionSpec as P
 
 
-EXTRA_ROWS = 16
+EXTRA_ROWS = 8
 
 
 def slot_numbers(route_ids, expert_count, capacity):
@@ -46,10 +46,12 @@
     down_dims = (((0,), (1,)), ((), ()))
     hidden_dims = (((1,), (1,)), ((), ()))
     features_here = activations.shape[0]
-    both = jnp.concatenate([activations, cotangent], axis=0)
-    send = jnp.dot(both, placing, preferred_element_type=jnp.float32).astype(jnp.bfloat16)
-    recv = lax.all_to_all(send, "expert", split_axis=1, concat_axis=1, tiled=True)
-    recv_in, recv_grad = recv[:features_here], recv[features_here:]
+    send_in = jnp.dot(activations, placing, preferred_element_type=jnp.float32).astype(jnp.bfloat16)
+    send_grad = jnp.dot(cotangent, placing, preferred_element_type=jnp.float32).astype(jnp.bfloat16)
+    recv_in, recv_grad = (
+        lax.all_to_all(send_in, "expert", split_axis=1, concat_axis=1, tiled=True),
+        lax.all_to_all(send_grad, "expert", split_axis=1, concat_axis=1, tiled=True),
+    )
     feature_piece = lax.all_gather(recv_in, "tensor", axis=0, tiled=True)
     grad_piece = lax.all_gather(recv_grad, "tensor", axis=0, tiled=True)
     gate_rows = gate_local
@@ -70,25 +72,14 @@
         up_rows, grad_up, hidden_dims, preferred_element_type=jnp.float32
     )
     tensor_count = lax.axis_size("tensor")
-    score_high = score_rows.astype(jnp.bfloat16)
-    score_low = (score_rows - score_high.astype(jnp.float32)).astype(jnp.bfloat16)
-    extra = jnp.concatenate(
-        [
-            score_high[None, :],
-            score_low[None, :],
-            jnp.zeros((EXTRA_ROWS - 2, slot_total), jnp.bfloat16),
-        ],
-        axis=0,
-    )
-    blocks = term.astype(jnp.bfloat16).reshape(tensor_count, features_here, slot_total)
-    extra = jnp.broadcast_to(extra[None], (tensor_count, EXTRA_ROWS, slot_total))
+    blocks = term.reshape(tensor_count, features_here, slot_total)
+    extra = jnp.broadcast_to(score_rows[None, None, :], (tensor_count, EXTRA_ROWS, slot_total))
     summed = lax.psum_scatter(
         jnp.concatenate([blocks, extra], axis=1), "tensor", scatter_dimension=0, tiled=False
     )
     back = lax.all_to_all(summed, "expert", split_axis=1, concat_axis=1, tiled=True)
-    back = back.astype(jnp.float32)
     back_terms = back[:features_here]
-    back_scores = back[features_here : features_here + 1] + back[features_here + 1 : features_here + 2]
+    back_scores = back[features_here : features_here + 1]
     grad_local = jnp.dot(
         back_terms, weighting.T, precision=lax.Precision.HIGHEST, preferred_element_type=jnp.float32
     )

time: 196 us -> 209 us (1.066)
  blocking collectives: 34.8 us -> 47.4 us
  local copies, waits for them, and re-layouts: 3.01 us -> 0.72 us
    reduce_scatter x1, waiting for transfers between devices: 43.8 us -> 56.7 us  [body(): lax.psum_scatter(jnp.concatenate([blocks, extra], axis=1), 'tensor', scat...]
    all_gather x1, waiting for transfers between devices: 26 us -> 14.9 us  [body(): feature_piece = lax.all_gather(recv_in, 'tensor', axis=0, tiled=True)]
    all_to_all x1, blocking collectives: 14.9 us -> 21.9 us  [body(): lax.all_to_all(summed, 'expert', split_axis=1, concat_axis=1, tiled=True)]
    all_to_all x1 -> x2, blocking collectives: 19.9 us -> 25.5 us  [the longest x1 14.7 us: body(): lax.all_to_all(send_in, 'expert', split_axis=1, concat_axis=1, tiled=True)]
  transfers between devices with their start and end apart: 3 -> 3, of which waited for: 3 -> 3; matrix products, arithmetic and copies ran while one was open for 9% -> 10% of each run, Pallas kernels for 0% -> 0%
where the time goes in v2:
time: 209 us
  waiting for transfers between devices  82 us (39%)
  matrix products  58.7 us (28%)
  blocking collectives  47.4 us (23%)
  between operations  13.8 us (7%)
  other arithmetic  5.74 us (3%)
    reduce_scatter x1, waiting for transfers between devices, body(): lax.psum_scatter(jnp.concatenate([blocks, extra], axis=1), 'tensor', scat...  56.7 us
    all_to_all x1, blocking collectives, body(): lax.all_to_all(summed, 'expert', split_axis=1, concat_axis=1, tiled=True)  21.9 us
    all_gather x1, waiting for transfers between devices, body(): feature_piece = lax.all_gather(recv_in, 'tensor', axis=0, tiled=True)  14.9 us
    all_to_all x1, blocking collectives, body(): lax.all_to_all(send_in, 'expert', split_axis=1, concat_axis=1, tiled=True)  14.7 us
    dot_general x1, matrix products, body(): lax.dot_general(gate_rows, grad_gate, hidden_dims, preferred_element_type...  12.8 us
    dot_general x1, matrix products, body(): lax.dot_general(grad_piece, down_local, down_dims, preferred_element_type...  12 us
    dot_general x1, matrix products, body(): lax.dot_general(up_rows, grad_up, hidden_dims, preferred_element_type=jnp...  11.5 us
    all_to_all x1, blocking collectives, body(): lax.all_to_all(send_grad, 'expert', split_axis=1, concat_axis=1, tiled=True)  10.7 us
  transfers between devices with their start and end apart: 3, of which 3 were waited for; matrix products, arithmetic and copies ran while one was open for 10% of the time, Pallas kernels for 0%

profile of v2, /device:TPU:0, one launch (start us, length us, event | category | flops | bytes accessed | tf_op | source)
XLA Modules:
  0.0 208.5 jit_solution(13532789780597607763)
XLA Ops:
  7.2 0.0 copy-start
  7.2 0.0 all-gather.5.cloned.1.call-start
  7.2 0.7 convert_reduce_fusion.1
  7.9 0.1 fusion.16
  8.1 0.7 select_reduce_fusion.2
  8.8 0.7 convert_add_fusion
  9.5 0.0 copy-done
  9.5 0.2 convolution_convert_fusion
  9.8 14.7 %all_to_all.33 = bf16[384,4,80]{0,2,1:T(8,128)(2,1)} all-to-all(bf16[384,4,80]{0,2,1:T(8,128)(2,1)S(1)} %bitcast.48), channel_id=1, replica_groups=mesh['expert'=4,'tensor'=8] {'expert'}, dimensions={1} | all-to-all | bytes 491520 | tf_op jit(solution)/shard_map/all_to_all | solution.py:52
  24.5 0.0 all-gather.5.cloned.1.call-update
  24.5 0.0 all-gather.3.cloned.1.call-start
  24.6 1.1 convolution_convert_fusion.1
  25.7 10.7 %all_to_all.34 = bf16[384,4,80]{0,2,1:T(8,128)(2,1)} all-to-all(bf16[384,4,80]{0,2,1:T(8,128)(2,1)S(1)} %bitcast.47), channel_id=1, replica_groups=mesh['expert'=4,'tensor'=8] {'expert'}, dimensions={1} | all-to-all | bytes 491520 | tf_op jit(solution)/shard_map/all_to_all | solution.py:53
  36.5 0.0 all-gather.3.cloned.1.call-update
  36.5 0.0 reduce-scatter.2.cloned.1.call-start
  36.5 14.9 %all-gather.5.cloned.1.call-done = bf16[3072,320]{0,1:T(8,128)(2,1)} async-done(((bf16[384,320]{0,1:T(8,128)(2,1)}), bf16[3072,320]{0,1:T(8,128)(2,1)}) %all-gather.5.cloned.1.call-update) | async-done | bytes 1966096 | tf_op jit(solution)/shard_map/all_gather | solution.py:55
  51.4 0.0 copy-start.3
  51.4 9.4 %fusion.2 = f32[320,2048]{1,0:T(8,128)S(1)} fusion(bf16[3072,320]{0,1:T(8,128)(2,1)} %all-gather.5.cloned.1.call-done, bf16[1,3072,2048]{2,1,0:T(8,128)(2,1)} %param.11), kind=kOutput, calls=%fused_computation.2 | convolution fusion | flops 4026531840 | bytes 17170432 | tf_op jit(solution)/shard_map/dot_general | solution.py:59
  60.8 0.0 copy-done.3
  60.8 0.0 copy-start.4
  60.8 9.8 %fusion.6 = f32[320,2048]{1,0:T(8,128)} fusion(bf16[3072,320]{0,1:T(8,128)(2,1)S(1)} %copy-done.3, bf16[1,3072,2048]{2,1,0:T(8,128)(2,1)} %param.12), kind=kOutput, calls=%fused_computation.6 | convolution fusion | flops 4026531840 | bytes 17170432 | tf_op jit(solution)/shard_map/dot_general | solution.py:62
  70.6 10.4 %all-gather.3.cloned.1.call-done = bf16[3072,320]{0,1:T(8,128)(2,1)} async-done(((bf16[384,320]{0,1:T(8,128)(2,1)}), bf16[3072,320]{0,1:T(8,128)(2,1)}) %all-gather.3.cloned.1.call-update) | async-done | bytes 1966096 | tf_op jit(solution)/shard_map/all_gather | solution.py:56
  80.9 12.0 %multiply_reduce_fusion = (f32[320]{0:T(512)S(1)}, f32[320,2048]{1,0:T(8,128)}) fusion(f32[320,2048]{1,0:T(8,128)} %fusion.6, f32[320,2048]{1,0:T(8,128)S(1)} %fusion.2, bf16[3072,320]{0,1:T(8,128)(2,1)} %all-gather.3.cloned.1.call-done, bf16[1,2048,3072]{2,1,0:T(8,128)(2,1)} %param.13), kind=kOutput, calls=%fused_computation.13 | convolution fusion | flops 4031119104 | bytes 22414592 | tf_op jit(solution)/shard_map/dot_general | solution.py:63
  92.9 0.0 copy-done.4
  92.9 12.8 %fusion = f32[320,3072]{1,0:T(8,128)} fusion(bf16[1,3072,2048]{2,1,0:T(8,128)(2,1)} %param.11, f32[320,2048]{1,0:T(8,128)S(1)} %fusion.2, f32[320,2048]{1,0:T(8,128)} %get-tuple-element.5, f32[320,2048]{1,0:T(8,128)} %fusion.6), kind=kOutput, calls=%fused_computation | convolution fusion | flops 4033085440 | bytes 24379392 | tf_op jit(solution)/shard_map/dot_general | solution.py:70
  105.7 11.5 %fusion.10 = f32[320,3072]{1,0:T(8,128)S(1)} fusion(f32[320,3072]{1,0:T(8,128)} %fusion, bf16[1,3072,2048]{2,1,0:T(8,128)(2,1)} %param.12, f32[320,2048]{1,0:T(8,128)} %get-tuple-element.5, f32[320,2048]{1,0:T(8,128)} %copy-done.4), kind=kOutput, calls=%fused_computation.11 | convolution fusion | flops 4031447040 | bytes 25690112 | tf_op jit(solution)/shard_map/dot_general | solution.py:71
  117.3 0.3 copy.21
  117.5 0.2 broadcast_in_dim.52
  117.7 2.9 %pad_maximum_fusion = f32[8,392,320]{1,2,0:T(8,128)} fusion(f32[8,8,320]{1,2,0:T(8,128)S(1)} %broadcast_in_dim.52, f32[8,384,320]{1,2,0:T(8,128)S(1)} %bitcast.42), kind=kLoop, calls=%fused_computation.10 | loop fusion | flops 1003520 | bytes 8028160 | tf_op jit(solution)/shard_map/concatenate | solution.py:78
  120.6 0.0 copy-start.2
  120.6 0.0 reduce-scatter.2.cloned.1.call-update
  120.6 0.0 copy-start.1
  120.6 56.7 %reduce-scatter.2.cloned.1.call-done = f32[1,392,320]{1,2,0:T(8,128)} async-done(((f32[8,392,320]{1,2,0:T(8,128)}), f32[1,392,320]{1,2,0:T(8,128)}) %reduce-scatter.2.cloned.1.call-update) | async-done | bytes 501776 | tf_op jit(solution)/shard_map/reduce_scatter | solution.py:77
  177.3 21.9 %all_to_all.35 = f32[392,4,80]{0,2,1:T(8,128)S(1)} all-to-all(f32[392,4,80]{0,2,1:T(8,128)} %bitcast.49), channel_id=1, replica_groups=mesh['expert'=4,'tensor'=8] {'expert'}, dimensions={1} | all-to-all | bytes 1003520 | tf_op jit(solution)/shard_map/all_to_all | solution.py:80
  199.2 0.2 slice_reduce_fusion
  199.4 0.1 broadcast_in_dim.55
  199.5 0.0 copy-done.2
  199.5 0.7 select_reduce_fusion
  200.2 1.8 convolution_convert_fusion.2
  202.0 0.0 copy-done.1
  (2 shorter events, 0.1 us)
Async XLA Ops:
  7.2 2.3 %copy-start = (bf16[384,128]{1,0:T(8,128)(2,1)S(1)}, bf16[384,128]{1,0:T(8,128)(2,1)}, u32[]{:S(2)}) copy-start(bf16[384,128]{1,0:T(8,128)(2,1)} %param.7) | copy-start | bytes 294916
  7.2 44.2 %all-gather.5.cloned.1.call-start = ((), (), s32[]{:S(2)}) async-start(), calls=%async_computation.5 | async-start | bytes 2211840 | tf_op jit(solution)/shard_map/all_gather | solution.py:55
  24.5 56.4 %all-gather.3.cloned.1.call-start = ((), (), s32[]{:S(2)}) async-start(), calls=%async_computation.4 | async-start | bytes 2211840 | tf_op jit(solution)/shard_map/all_gather | solution.py:56
  36.5 140.9 %reduce-scatter.2.cloned.1.call-start = ((), (), s32[]{:S(2)}) async-start(), calls=%async_computation.6 | async-start | bytes 5898240 | tf_op jit(solution)/shard_map/reduce_scatter | solution.py:77
  51.4 9.4 %copy-start.3 = (bf16[3072,320]{0,1:T(8,128)(2,1)S(1)}, bf16[3072,320]{0,1:T(8,128)(2,1)}, u32[]{:S(2)}) copy-start(bf16[3072,320]{0,1:T(8,128)(2,1)} %all-gather.5.cloned.1.call-done) | copy-start | bytes 5898244
  60.8 32.1 %copy-start.4 = (f32[320,2048]{1,0:T(8,128)}, f32[320,2048]{1,0:T(8,128)S(1)}, u32[]{:S(2)}) copy-start(f32[320,2048]{1,0:T(8,128)S(1)} %fusion.2) | copy-start | bytes 7864324
  120.6 78.9 %copy-start.2 = (f32[128,2]{0,1:T(2,128)S(1)}, f32[128,2]{0,1:T(2,128)}, u32[]{:S(2)}) copy-start(f32[128,2]{0,1:T(2,128)} %param.10) | copy-start | bytes 3076
  120.6 81.4 %copy-start.1 = (bf16[384,128]{1,0:T(8,128)(2,1)S(1)}, bf16[384,128]{1,0:T(8,128)(2,1)}, u32[]{:S(2)}) copy-start(bf16[384,128]{1,0:T(8,128)(2,1)} %param.7) | copy-start | bytes 294916
Sparse Core Ops, SparseCore 0:
  24.7 26.7 all-gather.4
  53.3 27.6 all-gather.2
  120.8 56.5 reduce-scatter.1

commit v3 on v1

--- a/solution.py
+++ b/solution.py
@@ -46,10 +46,12 @@
     down_dims = (((0,), (1,)), ((), ()))
     hidden_dims = (((1,), (1,)), ((), ()))
     features_here = activations.shape[0]
-    both = jnp.concatenate([activations, cotangent], axis=0)
-    send = jnp.dot(both, placing, preferred_element_type=jnp.float32).astype(jnp.bfloat16)
-    recv = lax.all_to_all(send, "expert", split_axis=1, concat_axis=1, tiled=True)
-    recv_in, recv_grad = recv[:features_here], recv[features_here:]
+    send_in = jnp.dot(activations, placing, preferred_element_type=jnp.float32).astype(jnp.bfloat16)
+    send_grad = jnp.dot(cotangent, placing, preferred_element_type=jnp.float32).astype(jnp.bfloat16)
+    recv_in, recv_grad = (
+        lax.all_to_all(send_in, "expert", split_axis=1, concat_axis=1, tiled=True),
+        lax.all_to_all(send_grad, "expert", split_axis=1, concat_axis=1, tiled=True),
+    )
     feature_piece = lax.all_gather(recv_in, "tensor", axis=0, tiled=True)
     grad_piece = lax.all_gather(recv_grad, "tensor", axis=0, tiled=True)
     gate_rows = gate_local
@@ -82,8 +84,21 @@
     )
     blocks = term.astype(jnp.bfloat16).reshape(tensor_count, features_here, slot_total)
     extra = jnp.broadcast_to(extra[None], (tensor_count, EXTRA_ROWS, slot_total))
-    summed = lax.psum_scatter(
-        jnp.concatenate([blocks, extra], axis=1), "tensor", scatter_dimension=0, tiled=False
+    parts = lax.all_to_all(
+        jnp.concatenate([blocks, extra], axis=1), "tensor", split_axis=0, concat_axis=0, tiled=True
+    ).astype(jnp.float32)
+    totals = jnp.sum(parts, axis=0)
+    score = totals[features_here : features_here + 1] + totals[features_here + 1 : features_here + 2]
+    score_high = score.astype(jnp.bfloat16)
+    score_low = (score - score_high.astype(jnp.float32)).astype(jnp.bfloat16)
+    summed = jnp.concatenate(
+        [
+            totals[:features_here].astype(jnp.bfloat16),
+            score_high,
+            score_low,
+            jnp.zeros((EXTRA_ROWS - 2, slot_total), jnp.bfloat16),
+        ],
+        axis=0,
     )
     back = lax.all_to_all(summed, "expert", split_axis=1, concat_axis=1, tiled=True)
     back = back.astype(jnp.float32)

time: 196 us -> 179 us (0.913)
  waiting for transfers between devices: 81.9 us -> 26.3 us
  blocking collectives: 34.8 us -> 73 us
    reduce_scatter x1 -> x0, waiting for transfers between devices: 43.8 us -> none  [body(): lax.psum_scatter(jnp.concatenate([blocks, extra], axis=1), 'tensor', scat...]
    all_to_all x1 -> x3, blocking collectives: 19.9 us -> 58.5 us  [the longest x1 33 us: body(): lax.all_to_all(jnp.concatenate([blocks, extra], axis=1), 'tensor', split_...]
    all_gather x1, waiting for transfers between devices: 26 us -> 14.9 us  [body(): feature_piece = lax.all_gather(recv_in, 'tensor', axis=0, tiled=True)]
  transfers between devices with their start and end apart: 3 -> 2, of which waited for: 3 -> 2; matrix products, arithmetic and copies ran while one was open for 9% -> 11% of each run, Pallas kernels for 0% -> 0%
where the time goes in v3:
time: 179 us; the launch traced here: 178 us
  blocking collectives  73 us (41%)
  matrix products  57.8 us (32%)
  waiting for transfers between devices  26.3 us (15%)
  between operations  14.2 us (8%)
  other arithmetic  3.87 us (2%)
  local copies, waits for them, and re-layouts  3.26 us (2%)
    all_to_all x1, blocking collectives, body(): lax.all_to_all(jnp.concatenate([blocks, extra], axis=1), 'tensor', split_...  33 us
    all_gather x1, waiting for transfers between devices, body(): feature_piece = lax.all_gather(recv_in, 'tensor', axis=0, tiled=True)  14.9 us
    all_to_all x1, blocking collectives, body(): lax.all_to_all(send_in, 'expert', split_axis=1, concat_axis=1, tiled=True)  14.7 us
    all_to_all x1, blocking collectives, body(): lax.all_to_all(summed, 'expert', split_axis=1, concat_axis=1, tiled=True)  14.5 us
    dot_general x1, matrix products, body(): lax.dot_general(gate_rows, grad_gate, hidden_dims, preferred_element_type...  12.8 us
    dot_general x1, matrix products, body(): lax.dot_general(up_rows, grad_up, hidden_dims, preferred_element_type=jnp...  12.1 us
    dot_general x1, matrix products, body(): lax.dot_general(grad_piece, down_local, down_dims, preferred_element_type...  12 us
    all_gather x1, waiting for transfers between devices, body(): grad_piece = lax.all_gather(recv_grad, 'tensor', axis=0, tiled=True)  11.3 us
  transfers between devices with their start and end apart: 2, of which 2 were waited for; matrix products, arithmetic and copies ran while one was open for 11% of the time, Pallas kernels for 0%

profile of v3, /device:TPU:0, one launch (start us, length us, event | category | flops | bytes accessed | tf_op | source)
XLA Modules:
  0.0 178.5 jit_solution(15263084820237573660)
XLA Ops:
  7.2 0.0 copy-start
  7.2 0.0 all-gather.5.cloned.1.call-start
  7.2 0.7 convert_reduce_fusion.2
  7.9 0.1 fusion.23
  8.1 0.7 select_reduce_fusion.2
  8.8 0.7 convert_add_fusion
  9.5 0.0 copy-done
  9.5 0.2 convolution_convert_fusion
  9.8 14.7 %all_to_all.38 = bf16[384,4,80]{0,2,1:T(8,128)(2,1)} all-to-all(bf16[384,4,80]{0,2,1:T(8,128)(2,1)S(1)} %bitcast.50), channel_id=1, replica_groups=mesh['expert'=4,'tensor'=8] {'expert'}, dimensions={1} | all-to-all | bytes 491520 | tf_op jit(solution)/shard_map/all_to_all | solution.py:52
  24.5 0.0 all-gather.5.cloned.1.call-update
  24.5 0.0 all-gather.3.cloned.1.call-start
  24.6 1.1 convolution_convert_fusion.1
  25.7 10.7 %all_to_all.39 = bf16[384,4,80]{0,2,1:T(8,128)(2,1)} all-to-all(bf16[384,4,80]{0,2,1:T(8,128)(2,1)S(1)} %bitcast.49), channel_id=1, replica_groups=mesh['expert'=4,'tensor'=8] {'expert'}, dimensions={1} | all-to-all | bytes 491520 | tf_op jit(solution)/shard_map/all_to_all | solution.py:53
  36.5 0.0 all-gather.3.cloned.1.call-update
  36.5 14.9 %all-gather.5.cloned.1.call-done = bf16[3072,320]{0,1:T(8,128)(2,1)} async-done(((bf16[384,320]{0,1:T(8,128)(2,1)}), bf16[3072,320]{0,1:T(8,128)(2,1)}) %all-gather.5.cloned.1.call-update) | async-done | bytes 1966096 | tf_op jit(solution)/shard_map/all_gather | solution.py:55
  51.4 0.0 copy-start.3
  51.4 9.4 %fusion.2 = f32[320,2048]{1,0:T(8,128)S(1)} fusion(bf16[3072,320]{0,1:T(8,128)(2,1)} %all-gather.5.cloned.1.call-done, bf16[1,3072,2048]{2,1,0:T(8,128)(2,1)} %param.11), kind=kOutput, calls=%fused_computation.2 | convolution fusion | flops 4026531840 | bytes 17170432 | tf_op jit(solution)/shard_map/dot_general | solution.py:59
  60.8 0.0 copy-done.3
  60.8 8.8 %fusion.6 = f32[320,2048]{1,0:T(8,128)} fusion(bf16[3072,320]{0,1:T(8,128)(2,1)S(1)} %copy-done.3, bf16[1,3072,2048]{2,1,0:T(8,128)(2,1)} %param.12), kind=kOutput, calls=%fused_computation.6 | convolution fusion | flops 4026531840 | bytes 17170432 | tf_op jit(solution)/shard_map/dot_general | solution.py:62
  69.6 11.3 %all-gather.3.cloned.1.call-done = bf16[3072,320]{0,1:T(8,128)(2,1)} async-done(((bf16[384,320]{0,1:T(8,128)(2,1)}), bf16[3072,320]{0,1:T(8,128)(2,1)}) %all-gather.3.cloned.1.call-update) | async-done | bytes 1966096 | tf_op jit(solution)/shard_map/all_gather | solution.py:56
  80.9 12.0 %multiply_reduce_fusion = (f32[320]{0:T(512)S(1)}, f32[320,2048]{1,0:T(8,128)}) fusion(f32[320,2048]{1,0:T(8,128)} %fusion.6, f32[320,2048]{1,0:T(8,128)S(1)} %fusion.2, bf16[3072,320]{0,1:T(8,128)(2,1)} %all-gather.3.cloned.1.call-done, bf16[1,2048,3072]{2,1,0:T(8,128)(2,1)} %param.13), kind=kOutput, calls=%fused_computation.14 | convolution fusion | flops 4031119104 | bytes 22414592 | tf_op jit(solution)/shard_map/dot_general | solution.py:63
  93.0 12.8 %fusion = f32[320,3072]{1,0:T(8,128)} fusion(bf16[1,3072,2048]{2,1,0:T(8,128)(2,1)} %param.11, f32[320,2048]{1,0:T(8,128)S(1)} %fusion.2, f32[320,2048]{1,0:T(8,128)} %get-tuple-element.7, f32[320,2048]{1,0:T(8,128)} %fusion.6), kind=kOutput, calls=%fused_computation | convolution fusion | flops 4033085440 | bytes 24379392 | tf_op jit(solution)/shard_map/dot_general | solution.py:70
  105.8 12.1 %fusion.16 = bf16[3072,320]{0,1:T(8,128)(2,1)} fusion(f32[320,3072]{1,0:T(8,128)} %fusion, bf16[1,3072,2048]{2,1,0:T(8,128)(2,1)} %param.12, f32[320,2048]{1,0:T(8,128)} %get-tuple-element.7, f32[320,2048]{1,0:T(8,128)S(1)} %fusion.2), kind=kOutput, calls=%fused_computation.13 | convolution fusion | flops 4032430080 | bytes 23724032 | tf_op jit(solution)/shard_map/dot_general | solution.py:71
  117.9 2.9 %copy.40 = bf16[3072,320]{1,0:T(8,128)(2,1)S(1)} copy(bf16[3072,320]{0,1:T(8,128)(2,1)} %fusion.16) | data formatting | bytes 3932160 | tf_op jit(solution)/shard_map/reshape | solution.py:85
  120.9 0.3 pad_maximum_fusion
  121.1 33.0 %all_to_all.40 = bf16[8,400,320]{2,1,0:T(8,128)(2,1)S(1)} all-to-all(bf16[8,400,320]{2,1,0:T(8,128)(2,1)S(1)} %pad_maximum_fusion), channel_id=1, replica_groups=mesh['expert'=4,'tensor'=8] {'tensor'}, dimensions={0} | all-to-all | bytes 4096000 | tf_op jit(solution)/shard_map/all_to_all | solution.py:87
  154.1 0.0 copy-start.1
  154.1 0.4 convert_reduce_fusion
  154.5 0.0 copy-start.2
  154.7 0.2 copy.39
  154.8 14.5 %all_to_all.41 = bf16[400,4,80]{0,2,1:T(8,128)(2,1)S(1)} all-to-all(bf16[400,4,80]{0,2,1:T(8,128)(2,1)S(1)} %bitcast.45), channel_id=1, replica_groups=mesh['expert'=4,'tensor'=8] {'expert'}, dimensions={1} | all-to-all | bytes 512000 | tf_op jit(solution)/shard_map/all_to_all | solution.py:103
  169.3 0.1 convert_element_type.115
  169.4 0.2 fusion.22
  169.6 0.1 broadcast_in_dim.57
  169.7 0.0 copy-done.2
  169.7 0.7 select_reduce_fusion
  170.4 1.2 convolution_convert_fusion.2
  171.6 0.0 copy-done.1
  (10 shorter events, 0.2 us)
Async XLA Ops:
  7.2 2.3 %copy-start = (bf16[384,128]{1,0:T(8,128)(2,1)S(1)}, bf16[384,128]{1,0:T(8,128)(2,1)}, u32[]{:S(2)}) copy-start(bf16[384,128]{1,0:T(8,128)(2,1)} %param.7) | copy-start | bytes 294916
  7.2 44.2 %all-gather.5.cloned.1.call-start = ((), (), s32[]{:S(2)}) async-start(), calls=%async_computation.5 | async-start | bytes 2211840 | tf_op jit(solution)/shard_map/all_gather | solution.py:55
  24.5 56.4 %all-gather.3.cloned.1.call-start = ((), (), s32[]{:S(2)}) async-start(), calls=%async_computation.4 | async-start | bytes 2211840 | tf_op jit(solution)/shard_map/all_gather | solution.py:56
  51.4 9.4 %copy-start.3 = (bf16[3072,320]{0,1:T(8,128)(2,1)S(1)}, bf16[3072,320]{0,1:T(8,128)(2,1)}, u32[]{:S(2)}) copy-start(bf16[3072,320]{0,1:T(8,128)(2,1)} %all-gather.5.cloned.1.call-done) | copy-start | bytes 5898244
  154.1 17.5 %copy-start.1 = (bf16[384,128]{1,0:T(8,128)(2,1)S(1)}, bf16[384,128]{1,0:T(8,128)(2,1)}, u32[]{:S(2)}) copy-start(bf16[384,128]{1,0:T(8,128)(2,1)} %param.7) | copy-start | bytes 294916
  154.5 15.2 %copy-start.2 = (f32[128,2]{0,1:T(2,128)S(1)}, f32[128,2]{0,1:T(2,128)}, u32[]{:S(2)}) copy-start(f32[128,2]{0,1:T(2,128)} %param.10) | copy-start | bytes 3076
Sparse Core Ops, SparseCore 0:
  24.7 26.7 all-gather.4
  53.3 27.6 all-gather.2

commit v4 on v3

--- a/solution.py
+++ b/solution.py
@@ -1,6 +1,8 @@
 import jax
 import jax.numpy as jnp
 from jax import lax
+from jax.experimental import pallas as pl
+from jax.experimental.pallas import tpu as pltpu
 from jax.sharding import PartitionSpec as P
 
 
@@ -18,15 +20,72 @@
     return route_ids * capacity + position
 
 
-def swiglu_backward(gate_sum, up_sum, hidden_grad):
-    sigma = jax.nn.sigmoid(gate_sum)
-    silu_value = gate_sum * sigma
+def hidden_kernel(gate_sum, up_sum, grads, gate, up, down, out, total, score):
+    step = pl.program_id(0)
+    blocks, features = total.shape[0], total.shape[1]
+
+    @pl.when(step == 0)
+    def _():
+        total[...] = jnp.zeros_like(total)
+        score[...] = jnp.zeros_like(score)
+
+    hidden_grad = jnp.dot(down[...], grads[...], preferred_element_type=jnp.float32)
+    a, b = gate_sum[...], up_sum[...]
+    sigma = jax.nn.sigmoid(a)
+    silu_value = a * sigma
     grad_up = (hidden_grad * silu_value).astype(jnp.bfloat16)
-    grad_gate = (hidden_grad * up_sum * sigma * (1.0 + gate_sum * (1.0 - sigma))).astype(
-        jnp.bfloat16
-    )
-    score_rows = jnp.sum(silu_value * up_sum * hidden_grad, axis=1)
-    return (grad_gate, grad_up, score_rows)
+    grad_gate = (hidden_grad * b * sigma * (1.0 + a * (1.0 - sigma))).astype(jnp.bfloat16)
+    score[...] += jnp.sum(silu_value * b * hidden_grad, axis=0, keepdims=True)
+
+    @pl.loop(0, blocks)
+    def _(block):
+        rows = pl.ds(pl.multiple_of(block * features, features), features)
+        total[block] += jnp.dot(
+            gate[rows, :], grad_gate, preferred_element_type=jnp.float32
+        ) + jnp.dot(up[rows, :], grad_up, preferred_element_type=jnp.float32)
+
+    @pl.when(step == pl.num_programs(0) - 1)
+    def _():
+        high = score[...].astype(jnp.bfloat16).astype(jnp.float32)
+        low = score[...] - high
+        row = lax.broadcasted_iota(jnp.int32, (EXTRA_ROWS, score.shape[1]), 0)
+        extra = jnp.where(row == 0, high, jnp.where(row == 1, low, 0.0)).astype(jnp.bfloat16)
+
+        @pl.loop(0, blocks)
+        def _(block):
+            out[block, :features, :] = total[block].astype(jnp.bfloat16)
+            out[block, features:, :] = extra
+
+
+def hidden_terms(gate_sum, up_sum, grads, gate, up, down, blocks):
+    hidden, slots = gate_sum.shape
+    depth = grads.shape[0]
+    tile = min(hidden, 256)
+    features = depth // blocks
+    return pl.pallas_call(
+        hidden_kernel,
+        grid=(hidden // tile,),
+        in_specs=[
+            pl.BlockSpec((tile, slots), lambda i: (i, 0)),
+            pl.BlockSpec((tile, slots), lambda i: (i, 0)),
+            pl.BlockSpec((depth, slots), lambda i: (0, 0)),
+            pl.BlockSpec((depth, tile), lambda i: (0, i)),
+            pl.BlockSpec((depth, tile), lambda i: (0, i)),
+            pl.BlockSpec((tile, depth), lambda i: (i, 0)),
+        ],
+        out_specs=pl.BlockSpec((blocks, features + EXTRA_ROWS, slots), lambda i: (0, 0, 0)),
+        out_shape=jax.ShapeDtypeStruct((blocks, features + EXTRA_ROWS, slots), jnp.bfloat16),
+        scratch_shapes=[
+            pltpu.VMEM((blocks, features, slots), jnp.float32),
+            pltpu.VMEM((1, slots), jnp.float32),
+        ],
+        compiler_params=pltpu.CompilerParams(vmem_limit_bytes=48 * 2**20),
+        cost_estimate=pl.CostEstimate(
+            flops=6 * hidden * depth * slots,
+            bytes_accessed=6 * hidden * depth,
+            transcendentals=hidden * slots,
+        ),
+    )(gate_sum, up_sum, grads, gate, up, down)
 
 
 def body(activations, cotangent, route_ids, gate_probs, gate_weight, up_weight, down_weight):
@@ -43,8 +102,6 @@
     up_local = up_weight[0]
     down_local = down_weight[0]
     first_dims = (((0,), (0,)), ((), ()))
-    down_dims = (((0,), (1,)), ((), ()))
-    hidden_dims = (((1,), (1,)), ((), ()))
     features_here = activations.shape[0]
     send_in = jnp.dot(activations, placing, preferred_element_type=jnp.float32).astype(jnp.bfloat16)
     send_grad = jnp.dot(cotangent, placing, preferred_element_type=jnp.float32).astype(jnp.bfloat16)
@@ -54,39 +111,15 @@
     )
     feature_piece = lax.all_gather(recv_in, "tensor", axis=0, tiled=True)
     grad_piece = lax.all_gather(recv_grad, "tensor", axis=0, tiled=True)
-    gate_rows = gate_local
-    up_rows = up_local
     gate_sum = lax.dot_general(
-        feature_piece, gate_rows, first_dims, preferred_element_type=jnp.float32
+        gate_local, feature_piece, first_dims, preferred_element_type=jnp.float32
     )
-    up_sum = lax.dot_general(feature_piece, up_rows, first_dims, preferred_element_type=jnp.float32)
-    hidden_grad = lax.dot_general(
-        grad_piece, down_local, down_dims, preferred_element_type=jnp.float32
+    up_sum = lax.dot_general(up_local, feature_piece, first_dims, preferred_element_type=jnp.float32)
+    terms = hidden_terms(
+        gate_sum, up_sum, grad_piece, gate_local, up_local, down_local, lax.axis_size("tensor")
     )
-    gate_sum, up_sum, hidden_grad = (gate_sum, up_sum, hidden_grad)
-    grad_gate, grad_up, score_rows = swiglu_backward(gate_sum, up_sum, hidden_grad)
-    gate_rows = gate_local
-    up_rows = up_local
-    term = lax.dot_general(gate_rows, grad_gate, hidden_dims, preferred_element_type=jnp.float32)
-    term = term + lax.dot_general(
-        up_rows, grad_up, hidden_dims, preferred_element_type=jnp.float32
-    )
-    tensor_count = lax.axis_size("tensor")
-    score_high = score_rows.astype(jnp.bfloat16)
-    score_low = (score_rows - score_high.astype(jnp.float32)).astype(jnp.bfloat16)
-    extra = jnp.concatenate(
-        [
-            score_high[None, :],
-            score_low[None, :],
-            jnp.zeros((EXTRA_ROWS - 2, slot_total), jnp.bfloat16),
-        ],
-        axis=0,
-    )
-    blocks = term.astype(jnp.bfloat16).reshape(tensor_count, features_here, slot_total)
-    extra = jnp.broadcast_to(extra[None], (tensor_count, EXTRA_ROWS, slot_total))
-    parts = lax.all_to_all(
-        jnp.concatenate([blocks, extra], axis=1), "tensor", split_axis=0, concat_axis=0, tiled=True
-    ).astype(jnp.float32)
+    parts = lax.all_to_all(terms, "tensor", split_axis=0, concat_axis=0, tiled=True)
+    parts = parts.astype(jnp.float32)
     totals = jnp.sum(parts, axis=0)
     score = totals[features_here : features_here + 1] + totals[features_here + 1 : features_here + 2]
     score_high = score.astype(jnp.bfloat16)

time: 179 us -> 179 us (level)
  Pallas kernels: 0 us -> 37.9 us
  blocking collectives: 73 us -> 37.8 us
  matrix products: 57.8 us -> 26.8 us
  waiting for transfers between devices: 26.3 us -> 51.3 us
  starting transfers between devices: 0.08 us -> 3.7 us
    pallas_call x0 -> x1, Pallas kernels: none -> 37.9 us  [hidden_terms(): pl.pallas_call(hidden_kernel, grid=(hidden // tile,), in_specs=[pl.BlockS...]
    all_to_all x1 -> x0, blocking collectives: 33 us -> none  [body(): lax.all_to_all(jnp.concatenate([blocks, extra], axis=1), 'tensor', split_...]
    dot_general x5 -> x2, matrix products: 55.1 us -> 24.1 us  [the longest x1 13.2 us: body(): lax.dot_general(up_local, feature_piece, first_dims, preferred_element_ty...]
    all_to_all x0 -> x1, waiting for transfers between devices: none -> 30.3 us  [body(): lax.all_to_all(terms, 'tensor', split_axis=0, concat_axis=0, tiled=True)]
    all_gather x1, waiting for transfers between devices: 11.3 us -> 6.83 us  [body(): grad_piece = lax.all_gather(recv_grad, 'tensor', axis=0, tiled=True)]
    all_to_all x0 -> x1, starting transfers between devices: none -> 3.62 us  [body(): lax.all_to_all(terms, 'tensor', split_axis=0, concat_axis=0, tiled=True)]
    reshape x1 -> x0, local copies, waits for them, and re-layouts: 2.9 us -> none  [body(): term.astype(jnp.bfloat16).reshape(tensor_count, features_here, slot_total)]
    all_to_all x1, blocking collectives: 14.5 us -> 12.4 us  [body(): lax.all_to_all(summed, 'expert', split_axis=1, concat_axis=1, tiled=True)]
  transfers between devices with their start and end apart: 2 -> 3, of which waited for: 2 -> 3; matrix products, arithmetic and copies ran while one was open for 11% -> 15% of each run, Pallas kernels for 0% -> 0%
where the time goes in v4:
time: 179 us; the launch traced here: 178 us
  waiting for transfers between devices  51.3 us (29%)
  Pallas kernels  37.9 us (21%)
  blocking collectives  37.8 us (21%)
  matrix products  26.8 us (15%)
  between operations  14.1 us (8%)
  starting transfers between devices  3.7 us (2%)
  other arithmetic  3.66 us (2%)
  local copies, waits for them, and re-layouts  2.98 us (2%)
    pallas_call x1, Pallas kernels, hidden_terms(): pl.pallas_call(hidden_kernel, grid=(hidden // tile,), in_specs=[pl.BlockS...  37.9 us
    all_to_all x1, waiting for transfers between devices, body(): lax.all_to_all(terms, 'tensor', split_axis=0, concat_axis=0, tiled=True)  30.3 us
    all_to_all x1, blocking collectives, body(): lax.all_to_all(send_in, 'expert', split_axis=1, concat_axis=1, tiled=True)  14.7 us
    all_gather x1, waiting for transfers between devices, body(): feature_piece = lax.all_gather(recv_in, 'tensor', axis=0, tiled=True)  14.1 us
    dot_general x1, matrix products, body(): lax.dot_general(up_local, feature_piece, first_dims, preferred_element_ty...  13.2 us
    all_to_all x1, blocking collectives, body(): lax.all_to_all(summed, 'expert', split_axis=1, concat_axis=1, tiled=True)  12.4 us
    dot_general x1, matrix products, body(): lax.dot_general(gate_local, feature_piece, first_dims, preferred_element_...  10.9 us
    all_to_all x1, blocking collectives, body(): lax.all_to_all(send_grad, 'expert', split_axis=1, concat_axis=1, tiled=True)  10.6 us
  transfers between devices with their start and end apart: 3, of which 3 were waited for; matrix products, arithmetic and copies ran while one was open for 15% of the time, Pallas kernels for 0%

profile of v4, /device:TPU:0, one launch (start us, length us, event | category | flops | bytes accessed | tf_op | source)
XLA Modules:
  0.0 178.3 jit_solution(1924736001297690817)
XLA Ops:
  7.2 0.0 copy-start
  7.2 0.0 all-gather.3.cloned.1.call-start
  7.2 0.7 convert_reduce_fusion.2
  7.9 0.1 fusion.1
  8.1 0.7 select_reduce_fusion.2
  8.8 0.7 convert_add_fusion
  9.5 0.0 copy-done
  9.5 0.2 convolution_convert_fusion.1
  9.8 14.7 %all_to_all.38 = bf16[384,4,80]{0,2,1:T(8,128)(2,1)} all-to-all(bf16[384,4,80]{0,2,1:T(8,128)(2,1)S(1)} %bitcast.38), channel_id=1, replica_groups=mesh['expert'=4,'tensor'=8] {'expert'}, dimensions={1} | all-to-all | bytes 491520 | tf_op jit(solution)/shard_map/all_to_all | solution.py:109
  24.5 0.0 all-gather.3.cloned.1.call-update
  24.5 0.0 all-gather.5.cloned.1.call-start
  24.6 1.1 convolution_convert_fusion
  25.7 10.6 %all_to_all.39 = bf16[384,4,80]{0,2,1:T(8,128)(2,1)S(1)} all-to-all(bf16[384,4,80]{0,2,1:T(8,128)(2,1)S(1)} %bitcast.36), channel_id=1, replica_groups=mesh['expert'=4,'tensor'=8] {'expert'}, dimensions={1} | all-to-all | bytes 491520 | tf_op jit(solution)/shard_map/all_to_all | solution.py:110
  36.3 0.9 copy.40
  37.3 0.0 all-gather.5.cloned.1.call-update
  37.3 14.1 %all-gather.3.cloned.1.call-done = bf16[3072,320]{0,1:T(8,128)(2,1)} async-done(((bf16[384,320]{0,1:T(8,128)(2,1)}), bf16[3072,320]{0,1:T(8,128)(2,1)}) %all-gather.3.cloned.1.call-update) | async-done | bytes 1966096 | tf_op jit(solution)/shard_map/all_gather | solution.py:112
  51.4 0.0 copy-start.3
  51.4 13.2 %convolution_bitcast_fusion.up_sum = f32[2048,320]{1,0:T(8,128)} fusion(bf16[3072,320]{0,1:T(8,128)(2,1)} %all-gather.3.cloned.1.call-done, bf16[1,3072,2048]{2,1,0:T(8,128)(2,1)} %param.12), kind=kOutput, calls=%fused_computation.1 | convolution fusion | flops 4026531840 | bytes 17170432 | tf_op jit(solution)/shard_map/dot_general | solution.py:117
  64.6 0.0 copy-done.3
  64.6 10.9 %convolution_bitcast_fusion.1.gate_sum = f32[2048,320]{1,0:T(8,128)} fusion(bf16[3072,320]{0,1:T(8,128)(2,1)S(1)} %copy-done.3, bf16[1,3072,2048]{2,1,0:T(8,128)(2,1)} %param.11), kind=kOutput, calls=%fused_computation.2 | convolution fusion | flops 4026531840 | bytes 17170432 | tf_op jit(solution)/shard_map/dot_general | solution.py:114
  75.5 6.8 %all-gather.5.cloned.1.call-done.grads = bf16[3072,320]{1,0:T(8,128)(2,1)} async-done(((bf16[384,320]{1,0:T(8,128)(2,1)}), bf16[3072,320]{1,0:T(8,128)(2,1)}) %all-gather.5.cloned.1.call-update) | async-done | bytes 1966096 | tf_op jit(solution)/shard_map/all_gather | solution.py:113
  82.3 0.0 copy-start.1
  82.3 1.7 copy-done.1
  84.0 37.9 %shard_map.86 = bf16[8,400,320]{2,1,0:T(8,128)(2,1)} custom-call(f32[2048,320]{1,0:T(8,128)} %convolution_bitcast_fusion.1.gate_sum, f32[2048,320]{1,0:T(8,128)} %convolution_bitcast_fusion.up_sum, bf16[3072,320]{1,0:T(8,128)(2,1)S(1)} %copy-done.1, bf16[3072,2048]{1,0:T(8,128)(2,1)} %bitcast.30, bf16[3072,2048]{1,0:T(8,128)(2,1)} %bitcast.31, ...), custom_call_target="tpu_custom_call" | custom-call | flops 12079595520 | bytes 37748736 | tf_op jit(solution)/shard_map/pallas_call | solution.py:65
  121.9 3.6 %all-to-all-start.2 = ((bf16[8,400,320]{2,1,0:T(8,128)(2,1)}), bf16[8,400,320]{2,1,0:T(8,128)(2,1)S(1)}, u32[]{:S(2)}, u32[]{:S(2)}) async-start(bf16[8,400,320]{2,1,0:T(8,128)(2,1)} %shard_map.86), calls=%async_computation.2 | async-start | bytes 4915200 | tf_op jit(solution)/shard_map/all_to_all | solution.py:121
  125.6 0.1 pad.3.clone
  125.7 0.0 copy-start.2
  125.7 30.3 %all-to-all-done.2 = bf16[8,400,320]{2,1,0:T(8,128)(2,1)S(1)} async-done(((bf16[8,400,320]{2,1,0:T(8,128)(2,1)}), bf16[8,400,320]{2,1,0:T(8,128)(2,1)S(1)}, u32[]{:S(2)}, u32[]{:S(2)}) %all-to-all-start.2) | async-done | bytes 2048032 | tf_op jit(solution)/shard_map/all_to_all | solution.py:121
  156.0 0.4 convert_reduce_fusion
  156.5 0.1 maximum_maximum_fusion
  156.6 0.2 copy.41
  156.8 12.4 %all_to_all.40 = bf16[400,4,80]{0,2,1:T(8,128)(2,1)S(1)} all-to-all(bf16[400,4,80]{0,2,1:T(8,128)(2,1)S(1)} %bitcast.33), channel_id=1, replica_groups=mesh['expert'=4,'tensor'=8] {'expert'}, dimensions={1} | all-to-all | bytes 512000 | tf_op jit(solution)/shard_map/all_to_all | solution.py:136
  169.2 0.1 convert_element_type.62
  169.2 0.2 fusion
  169.5 0.1 broadcast_in_dim.52
  169.6 0.0 copy-done.2
  169.6 0.7 select_reduce_fusion
  170.3 1.2 convolution_convert_fusion.2
  (5 shorter events, 0.1 us)
Async XLA Ops:
  7.2 2.3 %copy-start = (bf16[384,128]{1,0:T(8,128)(2,1)S(1)}, bf16[384,128]{1,0:T(8,128)(2,1)}, u32[]{:S(2)}) copy-start(bf16[384,128]{1,0:T(8,128)(2,1)} %param.7) | copy-start | bytes 294916
  7.2 44.2 %all-gather.3.cloned.1.call-start = ((), (), s32[]{:S(2)}) async-start(), calls=%async_computation.4 | async-start | bytes 2211840 | tf_op jit(solution)/shard_map/all_gather | solution.py:112
  24.5 57.8 %all-gather.5.cloned.1.call-start = ((), (), s32[]{:S(2)}) async-start(), calls=%async_computation.5 | async-start | bytes 2654208 | tf_op jit(solution)/shard_map/all_gather | solution.py:113
  51.4 13.2 %copy-start.3 = (bf16[3072,320]{0,1:T(8,128)(2,1)S(1)}, bf16[3072,320]{0,1:T(8,128)(2,1)}, u32[]{:S(2)}) copy-start(bf16[3072,320]{0,1:T(8,128)(2,1)} %all-gather.3.cloned.1.call-done) | copy-start | bytes 5898244
  82.3 1.7 copy-start.1
  121.9 34.1 %all-to-all-start.2 = ((bf16[8,400,320]{2,1,0:T(8,128)(2,1)}), bf16[8,400,320]{2,1,0:T(8,128)(2,1)S(1)}, u32[]{:S(2)}, u32[]{:S(2)}) async-start(bf16[8,400,320]{2,1,0:T(8,128)(2,1)} %shard_map.86), calls=%async_computation.2 | async-start | bytes 4915200 | tf_op jit(solution)/shard_map/all_to_all | solution.py:121
  125.7 43.9 %copy-start.2 = (f32[128,2]{0,1:T(2,128)S(1)}, f32[128,2]{0,1:T(2,128)}, u32[]{:S(2)}) copy-start(f32[128,2]{0,1:T(2,128)} %param.10) | copy-start | bytes 3076
Sparse Core Ops, SparseCore 0:
  24.7 26.7 all-gather.2
  53.3 29.0 all-gather.4
